TPU v7x, 256 devices: a whole 4x4x8 slice. The times are simulated.
256 devices in a mesh: pass: 64 (over y, z, core), tensor: 4 (over x).
Axes of the slice: x: 4, y: 4, z: 8, core: 2. Of those that a mesh axis runs over, the one named last changes fastest.
Arguments:
- queries: bfloat16 [8192, 4096], P('pass', 'tensor'), may hold values from -3 to 3
- keys_values: bfloat16 [128, 32, 2, 4096], P('pass', None, None, 'tensor'), may hold values from -4 to 4
- out_weight: bfloat16 [4096, 4096], P('tensor'), may hold values from -0.375 to 0.375
- cotangent: bfloat16 [8192, 4096], P('pass', 'tensor'), may hold values from -6 to 6
- retrieval: int32 [64, 32], replicated, may hold values from 0 to 127, as said below
- lengths: int32 [64], P('pass'), may hold values from 1 to 128
Outputs:
- attended: bfloat16 [8192, 4096], P('pass', 'tensor')
- grad_queries: bfloat16 [8192, 4096], P('pass', 'tensor')
- grad_keys_values: bfloat16 [128, 32, 2, 4096], P('pass', None, None, 'tensor')
Inputs may be any that keep to these rules, and one draw needn't show every extreme that they name: `retrieval`: row q lists 32 different passage ids; passage p is held by the device of index p // 2 along pass, and no row lists two passages of the same device.
All inputs are finite; a program needn't handle non-finite values.
Results may differ from a plain program's by a relative error of at most 0.015.
Values may be sent and summed in bfloat16 or wider, within the bound.
A program may use at most 128 MiB of HBM per device.

v0:
```python
import jax
import jax.numpy as jnp
from jax import lax
from jax.sharding import PartitionSpec as P

HS = 64


def local(queries, keys_values, out_weight, cotangent, retrieval, lengths):
    shard_count = lax.axis_size("pass")
    own_index = lax.axis_index("pass")
    per_shard = keys_values.shape[0]
    passage_len = keys_values.shape[1]
    tok_rows = queries.shape[0]
    head_cols = queries.shape[1]
    retrieved = retrieval.shape[1]
    key_count = retrieved * passage_len
    group_cols = 4 * HS
    group_count = head_cols // group_cols
    own_ids = lax.dynamic_index_in_dim(retrieval, own_index, 0, keepdims=False)
    own_shards = own_ids // per_shard
    matches = retrieval // per_shard == own_index
    holder = jnp.any(matches, axis=1)
    local_pick = jnp.sum(jnp.where(matches, retrieval % per_shard, 0), axis=1)
    selector = ((local_pick[:, None] == jnp.arange(per_shard)[None, :]) & holder[:, None]).astype(
        jnp.bfloat16
    )
    live_rows = jnp.arange(tok_rows) < lengths[0]
    masked_cot = jnp.where(live_rows[:, None], cotangent, jnp.zeros_like(cotangent))
    grad_context = lax.dot_general(
        lax.all_gather(masked_cot, "tensor", axis=1, tiled=True),
        out_weight,
        (((1,), (1,)), ((), ())),
        preferred_element_type=jnp.float32,
    ).astype(jnp.bfloat16)
    whole = lax.all_gather(keys_values, "pass", axis=0, tiled=True)
    picked = jnp.take(whole, own_ids, axis=0)
    passage_rows = picked.reshape(key_count, 2, head_cols)
    key_part = passage_rows[:, 0, :]
    value_part = passage_rows[:, 1, :]

    def group_terms(group):
        offset = group * group_cols
        query_slice = lax.dynamic_slice_in_dim(queries, offset, group_cols, 1).reshape(
            tok_rows, 4, HS
        )
        key_slice = lax.dynamic_slice_in_dim(key_part, offset, group_cols, 1).reshape(
            key_count, 4, HS
        )
        value_slice = lax.dynamic_slice_in_dim(value_part, offset, group_cols, 1).reshape(
            key_count, 4, HS
        )
        grad_slice = lax.dynamic_slice_in_dim(grad_context, offset, group_cols, 1).reshape(
            tok_rows, 4, HS
        )
        scores = jnp.einsum(
            "thd,rhd->htr", query_slice, key_slice, preferred_element_type=jnp.float32
        )
        row_max = jnp.max(scores, axis=-1, keepdims=True)
        raised = jnp.exp(scores - row_max)
        prob_full = raised / jnp.sum(raised, axis=-1, keepdims=True)
        prob_half = prob_full.astype(jnp.bfloat16)
        context = jnp.einsum(
            "htr,rhd->thd", prob_half, value_slice, preferred_element_type=jnp.float32
        )
        grad_prob = jnp.einsum(
            "thd,rhd->htr", grad_slice, value_slice, preferred_element_type=jnp.float32
        )
        grad_scores = prob_full * (
            grad_prob - jnp.sum(grad_prob * prob_full, axis=-1, keepdims=True)
        )
        grad_scores = grad_scores.astype(jnp.bfloat16)
        grad_query = jnp.einsum(
            "htr,rhd->thd", grad_scores, key_slice, preferred_element_type=jnp.float32
        )
        grad_key = jnp.einsum(
            "htr,thd->rhd", grad_scores, query_slice, preferred_element_type=jnp.float32
        )
        grad_value = jnp.einsum(
            "htr,thd->rhd", prob_half, grad_slice, preferred_element_type=jnp.float32
        )
        return (
            context.reshape(tok_rows, group_cols).astype(jnp.bfloat16),
            grad_query.reshape(tok_rows, group_cols).astype(jnp.bfloat16),
            grad_key.reshape(key_count, group_cols).astype(jnp.bfloat16),
            grad_value.reshape(key_count, group_cols).astype(jnp.bfloat16),
        )

    context_groups, query_groups, key_groups, value_groups = lax.map(
        group_terms, jnp.arange(group_count)
    )
    context = jnp.transpose(context_groups, (1, 0, 2)).reshape(tok_rows, head_cols)
    grad_queries = jnp.transpose(query_groups, (1, 0, 2)).reshape(tok_rows, head_cols)
    grad_keys = jnp.transpose(key_groups, (1, 0, 2)).reshape(key_count, head_cols)
    grad_values = jnp.transpose(value_groups, (1, 0, 2)).reshape(key_count, head_cols)
    mixed = jnp.dot(context, out_weight, preferred_element_type=jnp.float32)
    mixed = jnp.where(live_rows[:, None], mixed, 0.0)
    attended = lax.psum_scatter(
        mixed.astype(jnp.bfloat16), "tensor", scatter_dimension=1, tiled=True
    )
    slot_grads = jnp.stack([grad_keys, grad_values], axis=1).reshape(
        retrieved, passage_len, 2, head_cols
    )
    placement = (own_shards[:, None] == jnp.arange(shard_count)[None, :]).astype(jnp.bfloat16)
    outbound = jnp.einsum(
        "ks,klcf->slcf", placement, slot_grads, preferred_element_type=jnp.float32
    ).astype(jnp.bfloat16)
    returned = lax.all_to_all(outbound, "pass", split_axis=0, concat_axis=0, tiled=True)
    grad_keys_values = jnp.einsum(
        "op,olcf->plcf", selector, returned, preferred_element_type=jnp.float32
    ).astype(jnp.bfloat16)
    return (attended, grad_queries, grad_keys_values)


def solution(mesh):
    placed = (
        P("pass", "tensor"),
        P("pass", None, None, "tensor"),
        P("tensor", None),
        P("pass", "tensor"),
        P(),
        P("pass"),
    )
    return jax.shard_map(
        local,
        mesh=mesh,
        in_specs=placed,
        out_specs=(P("pass", "tensor"), P("pass", "tensor"), P("pass", None, None, "tensor")),
        check_vma=False,
    )
```

profile of v0, /device:TPU:2, one launch (start us, length us, event | category | flops | bytes accessed | tf_op | source)
XLA Modules:
  0.0 465.6 jit_solution(8245354408312763294)
XLA Ops:
  7.9 1.8 broadcast_select_fusion
  9.7 1.7 copy.34
  12.6 25.8 %all-gather.5.cloned.1.call-done = bf16[128,4096]{1,0:T(8,128)(2,1)} async-done(((bf16[128,1024]{1,0:T(8,128)(2,1)}), bf16[128,4096]{1,0:T(8,128)(2,1)}) %all-gather.5.cloned.1.call-update) | async-done | bytes 1048592 | tf_op jit(solution)/shard_map/all_gather | solution.py:31
  38.4 6.6 %convolution_convert_fusion.5 = bf16[128,1024]{1,0:T(8,128)(2,1)S(1)} fusion(bf16[128,4096]{1,0:T(8,128)(2,1)} %all-gather.5.cloned.1.call-done, bf16[1024,4096]{1,0:T(8,128)(2,1)} %param.10), kind=kOutput, calls=%fused_computation.33 | convolution fusion | flops 1073872896 | bytes 9699328 | tf_op jit(solution)/shard_map/dot_general | solution.py:30
  45.0 97.9 %all-gather.3.cloned.1.call-done = bf16[128,32,2,1024]{3,1,2,0:T(8,128)(2,1)} async-done(((bf16[2,32,2,1024]{3,1,2,0:T(8,128)(2,1)}), bf16[128,32,2,1024]{3,1,2,0:T(8,128)(2,1)}) %all-gather.3.cloned.1.call-update) | async-done | bytes 16777232 | tf_op jit(solution)/shard_map/all_gather | solution.py:36
  142.9 8.5 %gather_fusion = bf16[32,32,2,1024]{3,1,2,0:T(8,128)(2,1)} fusion(bf16[128,32,2,1024]{3,1,2,0:T(8,128)(2,1)} %all-gather.3.cloned.1.call-done, s32[1024]{0:T(1024)S(1)} %pad_clamp_fusion), kind=kCustom, calls=%fused_computation | custom fusion | bytes 8388736 | tf_op jit(solution)/shard_map/jit(_take)/gather | solution.py:37
  151.5 2.6 copy.35
  154.8 2.4 slice_bitcast_fusion
  157.2 56.5 %while.16 = (s32[]{:T(128)}, bf16[4,128,256]{1,2,0:T(8,128)(2,1)}, bf16[4,128,256]{1,2,0:T(8,128)(2,1)}, bf16[4,1024,256]{1,2,0:T(8,128)(2,1)}, bf16[4,1024,256]...) while((s32[]{:T(128)}, bf16[4,128,256]{1,2,0:T(8,128)(2,1)}, ...), condition=%wide.region_4.5_spmd, body=%wide.region_0.4_spmd.sunk | while | flops 545328640 | bytes 31735076 | solution.py:89
  158.4 1.1 constant_dynamic-slice_fusion.8
  159.8 0.9 constant_dynamic-slice_fusion.9
  161.6 1.1 constant_dynamic-slice_fusion.11
  162.7 1.0 copy.66
  163.9 1.6 multiply_reduce_fusion.2
  166.2 2.0 convolution_convert_fusion.12
  168.1 1.1 constant_dynamic-update-slice_fusion.7
  172.6 1.1 constant_dynamic-slice_fusion.8
  175.7 1.1 constant_dynamic-slice_fusion.11
  176.8 1.0 copy.66
  178.0 1.6 multiply_reduce_fusion.2
  180.3 2.0 convolution_convert_fusion.12
  182.3 1.1 constant_dynamic-update-slice_fusion.7
  186.7 1.1 constant_dynamic-slice_fusion.8
  188.0 0.9 constant_dynamic-slice_fusion.9
  189.9 1.1 constant_dynamic-slice_fusion.11
  191.0 1.0 copy.66
  192.1 1.6 multiply_reduce_fusion.2
  194.4 2.0 convolution_convert_fusion.12
  196.4 1.0 constant_dynamic-update-slice_fusion.7
  200.8 1.1 constant_dynamic-slice_fusion.8
  202.2 0.9 constant_dynamic-slice_fusion.9
  204.0 1.1 constant_dynamic-slice_fusion.11
  205.1 1.0 copy.66
  206.2 1.6 multiply_reduce_fusion.2
  208.6 2.0 convolution_convert_fusion.12
  210.5 1.1 constant_dynamic-update-slice_fusion.7
  213.7 3.0 copy.41
  216.8 2.7 stack.7
  219.5 2.7 copy.43
  222.3 4.3 copy.42
  226.5 4.5 stack.8
  231.0 2.7 copy.44
  233.7 2.7 convolution_convert_fusion.4
  236.5 17.9 %copy.45 = bf16[64,32,2,1024]{3,2,1,0:T(2,128)(2,1)} copy(bf16[64,32,2,1024]{3,0,2,1:T(8,128)(2,1)S(1)} %convolution_convert_fusion.4) | data formatting | bytes 16777216 | tf_op jit(solution)/shard_map/convert_element_type | solution.py:107
  254.4 6.6 %all-to-all-start = ((bf16[64,32,2,1024]{3,2,1,0:T(2,128)(2,1)}), bf16[64,32,2,1024]{3,2,1,0:T(2,128)(2,1)}, u32[]{:S(2)}, u32[]{:S(2)}) async-start(bf16[64,32,2,1024]{3,2,1,0:T(2,128)(2,1)} %copy.45), calls=%async_computation.1 | async-start | bytes 16777216 | tf_op jit(solution)/shard_map/all_to_all | solution.py:108
  261.3 5.7 %fusion.15 = bf16[128,4096]{1,0:T(8,128)(2,1)} fusion(bf16[128,1024]{0,1:T(8,128)(2,1)S(1)} %bitcast.129, bf16[1024,4096]{1,0:T(8,128)(2,1)} %param.10, pred[128]{0:T(512)(128)(4,1)S(1)} %iota_compare_fusion.1), kind=kOutput, calls=%fused_computation.25 | convolution fusion | flops 1074790400 | bytes 9699456 | tf_op jit(solution)/shard_map/dot_general | solution.py:96
  267.9 177.9 %all-to-all-done = bf16[64,32,2,1024]{3,2,1,0:T(2,128)(2,1)} async-done(((bf16[64,32,2,1024]{3,2,1,0:T(2,128)(2,1)}), bf16[64,32,2,1024]{3,2,1,0:T(2,128)(2,1)}, u32[]{:S(2)}, u32[]{:S(2)}) %all-to-all-start) | async-done | bytes 8388640 | tf_op jit(solution)/shard_map/all_to_all | solution.py:108
  445.9 12.3 %fusion.19 = bf16[2,32,2,1024]{3,0,2,1:T(2,128)(2,1)S(1)} fusion(bf16[64,32,2,1024]{3,2,1,0:T(2,128)(2,1)} %all-to-all-done, pred[64]{0:T(512)(128)(4,1)S(1)} %reduce_or.9, s32[64]{0:T(128)S(1)} %get-tuple-element.134), kind=kOutput, calls=%fused_computation.32 | convolution fusion | flops 16908544 | bytes 8651072 | tf_op jit(solution)/shard_map/op,olcf->plcf/dot_general | solution.py:109
  (100 shorter events, 23.4 us)
Async XLA Ops:
  7.2 31.2 %all-gather.5.cloned.1.call-start = ((), (), s32[]{:S(2)}) async-start(), calls=%async_computation.3 | async-start | bytes 1310720 | tf_op jit(solution)/shard_map/all_gather | solution.py:31
  9.7 133.3 %all-gather.3.cloned.1.call-start = ((), (), s32[]{:S(2)}) async-start(), calls=%async_computation.2 | async-start | bytes 17039360 | tf_op jit(solution)/shard_map/all_gather | solution.py:36
  159.7 4.0 copy-start
  168.1 1.2 copy-start.1
  168.1 1.6 copy-start.2
  173.9 4.0 copy-start
  182.3 1.2 copy-start.1
  182.3 1.6 copy-start.2
  188.0 4.0 copy-start
  196.4 1.2 copy-start.1
  196.4 1.6 copy-start.2
  202.1 4.0 copy-start
  210.5 1.2 copy-start.1
  210.5 1.6 copy-start.2
  254.4 6.8 %copy-start.3 = (bf16[4,128,256]{1,2,0:T(8,128)(2,1)S(1)}, bf16[4,128,256]{1,2,0:T(8,128)(2,1)}, u32[]{:S(2)}) copy-start(bf16[4,128,256]{1,2,0:T(8,128)(2,1)} %get-tuple-element.58) | copy-start | bytes 786436
  254.4 191.4 %all-to-all-start = ((bf16[64,32,2,1024]{3,2,1,0:T(2,128)(2,1)}), bf16[64,32,2,1024]{3,2,1,0:T(2,128)(2,1)}, u32[]{:S(2)}, u32[]{:S(2)}) async-start(bf16[64,32,2,1024]{3,2,1,0:T(2,128)(2,1)} %copy.45), calls=%async_computation.1 | async-start | bytes 16777216 | tf_op jit(solution)/shard_map/all_to_all | solution.py:108
  261.0 198.1 %reduce-scatter.2.cloned.1.call-start = ((), (), s32[]{:S(2)}) async-start(), calls=%async_computation.4 | async-start | bytes 1310720 | tf_op jit(solution)/shard_map/reduce_scatter | solution.py:98
  261.2 5.8 %copy-start.5 = (s32[64,32]{0,1:T(8,128)S(1)}, s32[64,32]{0,1:T(8,128)}, u32[]{:S(2)}) copy-start(s32[64,32]{0,1:T(8,128)} %param.12) | copy-start | bytes 24580
  261.3 5.8 %copy-start.4 = (bf16[4,128,256]{1,2,0:T(8,128)(2,1)S(1)}, bf16[4,128,256]{1,2,0:T(8,128)(2,1)}, u32[]{:S(2)}) copy-start(bf16[4,128,256]{1,2,0:T(8,128)(2,1)} %get-tuple-element.59) | copy-start | bytes 786436
Sparse Core Ops, SparseCore 0:
  9.8 28.5 all-gather.4
  41.7 101.1 all-gather.2
  267.1 24.8 reduce-scatter.1
where the time goes:
time: 469 us; the launch traced here: 466 us
  waiting for transfers between devices  302 us (64%)
  local copies, waits for them, and re-layouts  83.8 us (18%)
  matrix products  51.6 us (11%)
  between operations  14.5 us (3%)
  starting transfers between devices  6.9 us (1%)
    all_to_all x1, waiting for transfers between devices, local(): lax.all_to_all(outbound, 'pass', split_axis=0, concat_axis=0, tiled=True)  178 us
    all_gather x1, waiting for transfers between devices, local(): whole = lax.all_gather(keys_values, 'pass', axis=0, tiled=True)  97.9 us
    all_gather x1, waiting for transfers between devices, local(): lax.all_gather(masked_cot, 'tensor', axis=1, tiled=True)  25.8 us
    convert_element_type x1, local copies, waits for them, and re-layouts, local(): outbound = jnp.einsum('ks,klcf->slcf', placement, slot_grads, preferred_e...  17.9 us
    another operation x4, local copies, waits for them, and re-layouts, local(): jnp.stack([grad_keys, grad_values], axis=1)  12.7 us
    dot_general x1, matrix products, local(): jnp.einsum('op,olcf->plcf', selector, returned, preferred_element_type=jn...  12.3 us
    gather x2, local copies, waits for them, and re-layouts, local(): picked = jnp.take(whole, own_ids, axis=0)  11.1 us
  transfers between devices with their start and end apart: 4, of which 3 were waited for; matrix products, arithmetic and copies ran while one was open for 6% of the time, Pallas kernels for 0%

commit v1 on v0

v1 whole, which is shorter than its diff:
```python
import functools

import jax
import jax.numpy as jnp
from jax import lax
from jax.experimental import pallas as pl
from jax.experimental.pallas import tpu as pltpu
from jax.sharding import PartitionSpec as P

HS = 64
PAIR = 2 * HS
CORES = 2
CHUNKS = 4
MESH = pl.DeviceIdType.MESH
NT = (((1,), (1,)), ((), ()))
TN = (((0,), (0,)), ((), ()))
NN = (((1,), (0,)), ((), ()))


def dot(a, b, dims):
    return lax.dot_general(a, b, dims, preferred_element_type=jnp.float32)


def kernel(
    nx,
    ny,
    nz,
    ids_ref,
    inv_ref,
    len_ref,
    q_ref,
    kv_ref,
    w_ref,
    cot_ref,
    att_ref,
    gq_ref,
    gkv_ref,
    kvbuf,
    qbuf,
    gbuf,
    cotbuf,
    wbuf,
    gacc,
    gsend,
    kvg,
    ebuf,
    dsbuf,
    stbuf,
    ctxt,
    invl,
    csend,
    ctxbuf,
    qsend,
    sg,
    asend,
    arecv,
    aown,
    cxs,
    cxr,
    ysend,
    yrecv,
    ysum,
    zsend,
    loc_sem,
    kz_s,
    kz_r,
    ky_s,
    ky_r,
    kc_s,
    kc_r,
    q_s,
    q_r,
    g_s,
    g_r,
    c_s,
    c_r,
    d_s,
    d_r,
    x_s,
    x_r,
    a_s,
    a_r,
    e_s,
    e_r,
    f_s,
    f_r,
    o_s,
    o_r,
):
    nc = CORES
    rows = q_ref.shape[0]
    cols = q_ref.shape[1]
    pdev, plen, width = kv_ref.shape[1:]
    slots = ids_ref.shape[1]
    keys = slots * plen
    chunks = min(CHUNKS, nz)
    zper = nz // chunks
    me = lax.axis_index("pass")
    x = lax.axis_index("tensor")
    c = lax.rem(me, nc)
    z = lax.rem(me // nc, nz)
    y = me // (nc * nz)
    oc = 1 - c

    def at(yy, zz, cc):
        return (yy * nz + zz) * nc + cc

    def turn(t):
        half = (t + 1) // 2
        return jnp.where(lax.rem(t, 2) == 1, half, -half)

    def zat(t):
        return lax.rem(z + turn(t) + nz, nz)

    def yat(t):
        return lax.rem(y + turn(t) + ny, ny)

    def xat(t):
        return lax.rem(x + turn(t) + nx, nx)

    def place(yy, cc, zz):
        return ((yy * nc + cc) * nz + zz) * pdev

    def remote(src, dst, send, recv, dev):
        return pltpu.make_async_remote_copy(
            src_ref=src,
            dst_ref=dst,
            send_sem=send,
            recv_sem=recv,
            device_id=dev,
            device_id_type=MESH,
        )

    def each(lo, hi, body):
        lax.fori_loop(lo, hi, lambda t, carry: (body(t), carry)[1], 0)

    def lanes(i):
        return pl.ds(pl.multiple_of(i * PAIR, PAIR), PAIR)

    def kz_copy(zt, zs):
        return remote(
            kv_ref.at[zt],
            kvbuf.at[pl.ds(place(y, c, zs), pdev)],
            kz_s.at[zt],
            kz_r.at[zs],
            (at(y, zt, c), x),
        )

    def ky_copy(yt, ys, i):
        part = pl.ds(place(ys, c, i * zper), zper * pdev)
        return remote(
            kvbuf.at[part],
            kvbuf.at[part],
            ky_s.at[yt * chunks + i],
            ky_r.at[ys * chunks + i],
            (at(yt, z, c), x),
        )

    def kc_copy(ys, cs, i):
        part = pl.ds(place(ys, cs, i * zper), zper * pdev)
        return remote(
            kvbuf.at[part],
            kvbuf.at[part],
            kc_s.at[ys * chunks + i],
            kc_r.at[ys * chunks + i],
            (at(y, z, oc), x),
        )

    def q_copy(zt, zs):
        return remote(
            q_ref.at[:, lanes(zt)], qbuf.at[zs], q_s.at[zt], q_r.at[zs], (at(y, zt, c), x)
        )

    def g_copy(zt, zs):
        return remote(
            gsend.at[zt], gbuf.at[zs], g_s.at[zt], g_r.at[zs], (at(y, zt, c), x)
        )

    def c_copy(zt, zs):
        return remote(
            csend.at[zt], ctxbuf.at[:, lanes(zs)], c_s.at[zt], c_r.at[zs], (at(y, zt, c), x)
        )

    def d_copy(zt, zs):
        return remote(
            qsend.at[zt], gq_ref.at[:, lanes(zs)], d_s.at[zt], d_r.at[zs], (at(y, zt, c), x)
        )

    def x_copy(xt, xs):
        return remote(cot_ref, cotbuf.at[xs], x_s.at[xt], x_r.at[xs], (me, xt))

    def a_copy(xt, xs):
        return remote(asend.at[xt], arecv.at[xs], a_s.at[xt], a_r.at[xs], (me, xt))

    def e_copy(yt):
        return remote(cxs.at[yt], cxr.at[yt], e_s.at[yt], e_r.at[yt], (at(y, z, oc), x))

    def f_copy(yt, ys):
        return remote(ysend.at[yt], yrecv.at[ys], f_s.at[yt], f_r.at[ys], (at(yt, z, c), x))

    def o_copy(zt, zs):
        return remote(zsend.at[zt], gkv_ref.at[zs], o_s.at[zt], o_r.at[zs], (at(y, zt, c), x))

    w_load = pltpu.make_async_copy(w_ref, wbuf, loc_sem.at[0])
    kv_own = pltpu.make_async_copy(
        kv_ref.at[z], kvbuf.at[pl.ds(place(y, c, z), pdev)], loc_sem.at[1]
    )
    q_own = pltpu.make_async_copy(q_ref.at[:, lanes(z)], qbuf.at[z], loc_sem.at[2])
    cot_own = pltpu.make_async_copy(cot_ref, cotbuf.at[x], loc_sem.at[3])
    gq_own = pltpu.make_async_copy(qsend.at[z], gq_ref.at[:, lanes(z)], loc_sem.at[4])
    gkv_own = pltpu.make_async_copy(zsend.at[z], gkv_ref.at[z], loc_sem.at[5])

    barrier = pltpu.get_barrier_semaphore()

    def greet(dev):
        pl.semaphore_signal(barrier, inc=1, device_id=dev, device_id_type=MESH)

    each(1, nz, lambda t: greet((at(y, zat(t), c), x)))
    each(1, ny, lambda t: greet((at(yat(t), z, c), x)))
    each(1, nx, lambda t: greet((me, xat(t))))
    greet((at(y, z, oc), x))
    kv_own.start()
    cot_own.start()
    q_own.start()
    w_load.start()
    pl.semaphore_wait(barrier, nz + ny + nx - 2)

    each(1, nx, lambda t: x_copy(xat(t), x).start())
    each(1, nz, lambda t: kz_copy(zat(t), z).start())
    each(1, nz, lambda t: q_copy(zat(t), z).start())

    live = lax.broadcasted_iota(jnp.int32, (rows, 1), 0) < len_ref[0]
    low_lane = lax.broadcasted_iota(jnp.int32, (1, PAIR), 1) < HS
    low_row = lax.broadcasted_iota(jnp.int32, (PAIR, 1), 0) < HS
    blank = jnp.zeros((1, 1), jnp.bfloat16)

    sg_zero = jnp.zeros((plen, width), jnp.bfloat16)

    def clear(j):
        sg[j, slots] = sg_zero

    each(0, nz, clear)

    step = 256
    cot_own.wait()
    w_load.wait()

    def grad_part(xs, first):
        block = cotbuf[xs]

        def one(n):
            at_n = pl.ds(pl.multiple_of(n * step, step), step)
            weight = wbuf[at_n, pl.ds(pl.multiple_of(xs * cols, cols), cols)]
            part = dot(block, weight, NT)
            if first:
                gacc[:, at_n] = part
            else:
                gacc[:, at_n] += part

        each(0, cols // step, one)

    grad_part(x, True)

    kv_own.wait()

    def forward(i):
        def arrived(k):
            zs = i * zper + k

            @pl.when(zs != z)
            def _():
                kz_copy(zs, zs).wait_recv()

        each(0, zper, arrived)
        each(1, ny, lambda t: ky_copy(yat(t), y, i).start())
        kc_copy(y, c, i).start()

    each(0, chunks, forward)

    def other_part(t):
        xs = xat(t)
        x_copy(xs, xs).wait_recv()
        grad_part(xs, False)

    each(1, nx, other_part)
    for h in range(nz):
        gsend[h] = jnp.where(live, gacc[:, h * PAIR : (h + 1) * PAIR], 0.0).astype(jnp.bfloat16)
    gbuf[z] = gsend[z]
    each(1, nz, lambda t: g_copy(zat(t), z).start())

    def pass_on(t):
        ys = yat(t)

        def one(i):
            ky_copy(ys, ys, i).wait_recv()
            kc_copy(ys, c, i).start()

        each(0, chunks, one)

    each(1, ny, pass_on)
    each(0, ny * chunks, lambda k: kc_copy(k // chunks, oc, lax.rem(k, chunks)).wait_recv())

    q_own.wait()
    tile = 256
    tiles = keys // tile

    def both_rows(block):
        return jnp.concatenate(
            [jnp.where(low_lane, block, blank), jnp.where(low_lane, blank, block)], axis=0
        )

    def both_cols(block):
        return jnp.concatenate(
            [jnp.where(low_row, block, blank), jnp.where(low_row, blank, block)], axis=1
        )

    def pick(wide):
        return jnp.where(low_row, wide[:, :rows], wide[:, rows:])

    def attend(t):
        j = zat(t)

        @pl.when(t > 0)
        def _():
            q_copy(j, j).wait_recv()

        for k in range(slots):
            kvg[j, k * plen : (k + 1) * plen, :] = kvbuf[ids_ref[j, k]]
        query = both_rows(qbuf[j])
        top = jnp.full((1, 2 * rows), -jnp.inf, jnp.float32)
        for r in range(tiles):
            at_r = pl.ds(r * tile, tile)
            part = dot(kvg[j, at_r, :PAIR], query, NT)
            stbuf[at_r, :] = part
            top = jnp.maximum(top, jnp.max(part, axis=0, keepdims=True))
        total = jnp.zeros((1, 2 * rows), jnp.float32)
        for r in range(tiles):
            at_r = pl.ds(r * tile, tile)
            raised = jnp.exp(stbuf[at_r, :] - top)
            total = total + jnp.sum(raised, axis=0, keepdims=True)
            ebuf[j, at_r, :] = raised.astype(jnp.bfloat16)
        inverse = 1.0 / total
        mixed = dot(kvg[j, :, PAIR:], ebuf[j], TN) * inverse
        mixed = pick(mixed)
        ctxt[j] = mixed
        invl[j] = inverse
        csend[j] = mixed.T.astype(jnp.bfloat16)

        @pl.when(t > 0)
        def _():
            c_copy(j, z).start()

    each(0, nz, attend)
    ctxbuf[:, lanes(z)] = csend[z]

    def grads(t):
        j = zat(t)

        @pl.when(t > 0)
        def _():
            g_copy(j, j).wait_recv()

        query = both_rows(qbuf[j])
        inverse = jnp.where(low_row, invl[j, :, :rows], invl[j, :, rows:])
        scaled = gbuf[j].astype(jnp.float32).T * inverse
        product = scaled * ctxt[j]
        delta = jnp.concatenate(
            [
                jnp.sum(product[:HS], axis=0, keepdims=True),
                jnp.sum(product[HS:], axis=0, keepdims=True),
            ],
            axis=1,
        )
        wide = both_cols(scaled.astype(jnp.bfloat16))
        for r in range(tiles):
            at_r = pl.ds(r * tile, tile)
            raised = ebuf[j, at_r, :]
            grad = dot(kvg[j, at_r, PAIR:], wide, NN)
            grad = (raised.astype(jnp.float32) * (grad - delta)).astype(jnp.bfloat16)
            dsbuf[at_r, :] = grad
            per = tile // plen
            key_grad = dot(grad, query, NN).astype(jnp.bfloat16)
            value_grad = dot(raised, wide, NT).astype(jnp.bfloat16)
            sg[j, r * per : (r + 1) * per, :, :PAIR] = key_grad.reshape(per, plen, PAIR)
            sg[j, r * per : (r + 1) * per, :, PAIR:] = value_grad.reshape(per, plen, PAIR)
        back = pick(dot(kvg[j, :, :PAIR], dsbuf[...], TN))
        qsend[j] = back.T.astype(jnp.bfloat16)

        @pl.when(t > 0)
        def _():
            d_copy(j, z).start()

    each(0, nz // 2, grads)

    each(1, nz, lambda t: c_copy(zat(t), zat(t)).wait_recv())

    def project(xt, own):
        def one(n):
            at_n = pl.ds(pl.multiple_of(n * step, step), step)
            weight = wbuf[:, pl.ds(pl.multiple_of(xt * cols + n * step, step), step)]
            part = jnp.where(live, dot(ctxbuf[...], weight, NN), 0.0)
            if own:
                aown[:, at_n] = part
            else:
                asend[xt, :, at_n] = part.astype(jnp.bfloat16)

        each(0, cols // step, one)

    def project_other(t):
        xt = xat(t)
        project(xt, False)
        a_copy(xt, x).start()

    each(1, nx, project_other)
    project(x, True)
    each(nz // 2, nz, grads)
    gq_own.start()

    def gather(p):
        total = sg[0, inv_ref[0, p]].astype(jnp.float32)
        for j in range(1, nz):
            total = total + sg[j, inv_ref[j, p]].astype(jnp.float32)
        return total

    per_y = nz * pdev

    def for_other_core(t):
        yt = yat(ny - 1 - t)

        def one(k):
            cxs[yt, k] = gather(place(yt, oc, 0) + k).astype(jnp.bfloat16)

        each(0, per_y, one)
        e_copy(yt).start()

    each(0, ny, for_other_core)

    def for_other_y(t):
        yt = yat(t)
        e_copy(yt).wait_recv()

        def one(k):
            total = gather(place(yt, c, 0) + k) + cxr[yt, k].astype(jnp.float32)
            ysend[yt, k] = total.astype(jnp.bfloat16)

        each(0, per_y, one)
        f_copy(yt, y).start()

    each(1, ny, for_other_y)
    e_copy(y).wait_recv()

    def own_y(k):
        ysum[k] = gather(place(y, c, 0) + k) + cxr[y, k].astype(jnp.float32)

    each(0, per_y, own_y)

    each(1, nx, lambda t: a_copy(xat(t), xat(t)).wait_recv())
    out = aown[...]
    for t in range(1, nx):
        out = out + arecv[xat(t)].astype(jnp.float32)
    att_ref[...] = out.astype(jnp.bfloat16)

    each(1, ny, lambda t: f_copy(yat(t), yat(t)).wait_recv())

    def finish(t):
        zt = zat(t)
        for k in range(pdev):
            total = ysum[zt * pdev + k]
            for s in range(1, ny):
                total = total + yrecv[yat(s), zt * pdev + k].astype(jnp.float32)
            zsend[zt, k] = total.astype(jnp.bfloat16)

        @pl.when(t > 0)
        def _():
            o_copy(zt, z).start()

    each(0, nz, lambda t: finish(nz - 1 - t))
    gkv_own.start()

    gq_own.wait()
    gkv_own.wait()

    def settle_z(t):
        zt = zat(t)
        d_copy(zt, zt).wait_recv()
        o_copy(zt, zt).wait_recv()
        kz_copy(zt, z).wait_send()
        q_copy(zt, z).wait_send()
        g_copy(zt, z).wait_send()
        c_copy(zt, z).wait_send()
        d_copy(zt, z).wait_send()
        o_copy(zt, z).wait_send()

    each(1, nz, settle_z)

    def settle_y(t):
        each(0, chunks, lambda i: ky_copy(yat(t), y, i).wait_send())
        f_copy(yat(t), y).wait_send()

    each(1, ny, settle_y)
    each(0, ny * chunks, lambda k: kc_copy(k // chunks, c, lax.rem(k, chunks)).wait_send())
    each(0, ny, lambda t: e_copy(t).wait_send())

    def settle_x(t):
        x_copy(xat(t), x).wait_send()
        a_copy(xat(t), x).wait_send()

    each(1, nx, settle_x)


def local(queries, keys_values, out_weight, cotangent, retrieval, lengths):
    pass_count = lax.axis_size("pass")
    nx = lax.axis_size("tensor")
    me = lax.axis_index("pass")
    pdev, plen, _, cols = keys_values.shape
    rows = queries.shape[0]
    width = out_weight.shape[1]
    slots = retrieval.shape[1]
    nz = cols // PAIR
    ny = pass_count // (nz * CORES)
    passages = pass_count * pdev
    keys = slots * plen

    own = lax.dynamic_slice(
        retrieval.reshape(ny, nz, CORES, slots),
        (me // (nz * CORES), 0, me % CORES, 0),
        (1, nz, 1, slots),
    ).reshape(nz, slots)
    holder = own // pdev
    hy, hz, hc = holder // (nz * CORES), (holder // CORES) % nz, holder % CORES
    ids = ((hy * CORES + hc) * nz + hz) * pdev + own % pdev
    match = ids[:, :, None] == jnp.arange(passages)[None, None, :]
    inverse = slots + jnp.sum(
        jnp.where(match, jnp.arange(slots)[None, :, None] - slots, 0), axis=1
    )
    pairs = (
        keys_values.reshape(pdev, plen, 2, nz, PAIR)
        .transpose(3, 0, 1, 2, 4)
        .reshape(nz, pdev, plen, 2 * PAIR)
    )

    bf, f32 = jnp.bfloat16, jnp.float32
    chunks = min(CHUNKS, nz)
    dma = pltpu.SemaphoreType.DMA
    vmem = pltpu.VMEM
    attended, grad_queries, grad_pairs = pl.pallas_call(
        functools.partial(kernel, nx, ny, nz),
        out_shape=(
            jax.ShapeDtypeStruct((rows, cols), bf),
            jax.ShapeDtypeStruct((rows, cols), bf),
            jax.ShapeDtypeStruct((nz, pdev, plen, 2 * PAIR), bf),
        ),
        in_specs=[pl.BlockSpec(memory_space=pltpu.SMEM)] * 3
        + [pl.BlockSpec(memory_space=pl.ANY)] * 4,
        out_specs=(
            pl.BlockSpec(memory_space=pltpu.VMEM),
            pl.BlockSpec(memory_space=pl.ANY),
            pl.BlockSpec(memory_space=pl.ANY),
        ),
        scratch_shapes=[
            vmem((passages, plen, 2 * PAIR), bf),
            vmem((nz, rows, PAIR), bf),
            vmem((nz, rows, PAIR), bf),
            vmem((nx, rows, cols), bf),
            vmem((cols, width), bf),
            vmem((rows, cols), f32),
            vmem((nz, rows, PAIR), bf),
            vmem((nz, keys, 2 * PAIR), bf),
            vmem((nz, keys, 2 * rows), bf),
            vmem((keys, 2 * rows), bf),
            vmem((keys, 2 * rows), f32),
            vmem((nz, PAIR, rows), f32),
            vmem((nz, 1, 2 * rows), f32),
            vmem((nz, rows, PAIR), bf),
            vmem((rows, cols), bf),
            vmem((nz, rows, PAIR), bf),
            vmem((nz, slots + 1, plen, 2 * PAIR), bf),
            vmem((nx, rows, cols), bf),
            vmem((nx, rows, cols), bf),
            vmem((rows, cols), f32),
            vmem((ny, nz * pdev, plen, 2 * PAIR), bf),
            vmem((ny, nz * pdev, plen, 2 * PAIR), bf),
            vmem((ny, nz * pdev, plen, 2 * PAIR), bf),
            vmem((ny, nz * pdev, plen, 2 * PAIR), bf),
            vmem((nz * pdev, plen, 2 * PAIR), f32),
            vmem((nz, pdev, plen, 2 * PAIR), bf),
            dma((6,)),
        ]
        + [dma((nz,))] * 2
        + [dma((ny * chunks,))] * 4
        + [dma((nz,))] * 8
        + [dma((nx,))] * 4
        + [dma((ny,))] * 4
        + [dma((nz,))] * 2,
        compiler_params=pltpu.CompilerParams(
            collective_id=0, has_side_effects=True, vmem_limit_bytes=48 * 1024 * 1024
        ),
    )(ids, inverse, lengths, queries, pairs, out_weight, cotangent)
    grad_keys_values = (
        grad_pairs.reshape(nz, pdev, plen, 2, PAIR)
        .transpose(1, 2, 3, 0, 4)
        .reshape(pdev, plen, 2, cols)
    )
    return (attended, grad_queries, grad_keys_values)


def solution(mesh):
    placed = (
        P("pass", "tensor"),
        P("pass", None, None, "tensor"),
        P("tensor", None),
        P("pass", "tensor"),
        P(),
        P("pass"),
    )
    return jax.shard_map(
        local,
        mesh=mesh,
        in_specs=placed,
        out_specs=(P("pass", "tensor"), P("pass", "tensor"), P("pass", None, None, "tensor")),
        check_vma=False,
    )
```

time: 469 us -> 86.3 us (0.18)
  waiting for transfers between devices: 302 us -> 0 us
  local copies, waits for them, and re-layouts: 83.8 us -> 5.47 us
  Pallas kernels: 0 us -> 77.9 us
  matrix products: 51.6 us -> 0 us
  between operations: 14.5 us -> 1.43 us
  starting transfers between devices: 6.9 us -> 0 us
    all_to_all x1 -> x0, waiting for transfers between devices: 178 us -> none  [local(): lax.all_to_all(outbound, 'pass', split_axis=0, concat_axis=0, tiled=True)]
    all_gather x2 -> x0, waiting for transfers between devices: 124 us -> none  [the longest x1 97.9 us: local(): whole = lax.all_gather(keys_values, 'pass', axis=0, tiled=True)]
    pallas_call x0 -> x1, Pallas kernels: none -> 77.9 us  [local(): pl.pallas_call(functools.partial(kernel, nx, ny, nz), out_shape=(jax.Shap...]
    dot_general x24 -> x0, matrix products: 48.3 us -> none  [the longest x1 12.3 us: local(): jnp.einsum('op,olcf->plcf', selector, returned, preferred_element_type=jn...]
    dynamic_slice x37 -> x1, local copies, waits for them, and re-layouts: 21.4 us -> 0.01 us  [local(): lax.dynamic_slice(retrieval.reshape(ny, nz, CORES, slots), (me // (nz * C...]
    convert_element_type x1 -> x0, local copies, waits for them, and re-layouts: 17.9 us -> none  [local(): outbound = jnp.einsum('ks,klcf->slcf', placement, slot_grads, preferred_e...]
    another operation x4 -> x0, local copies, waits for them, and re-layouts: 12.7 us -> none  [local(): jnp.stack([grad_keys, grad_values], axis=1)]
    gather x2 -> x0, local copies, waits for them, and re-layouts: 11.1 us -> none  [local(): picked = jnp.take(whole, own_ids, axis=0)]
  transfers between devices with their start and end apart: 4 -> 0, of which waited for: 3 -> 0; matrix products, arithmetic and copies ran while one was open for 6% -> 0% of each run, Pallas kernels for 0% -> 0%
where the time goes in v1:
time: 86.3 us; the launch traced here: 84.9 us
  Pallas kernels  77.9 us (90%)
  local copies, waits for them, and re-layouts  5.47 us (6%)
  between operations  1.43 us (2%)
    pallas_call x1, Pallas kernels, local(): pl.pallas_call(functools.partial(kernel, nx, ny, nz), out_shape=(jax.Shap...  77.9 us
    unnamed x9, local copies, waits for them, and re-layouts  4.11 us

profile of v1, /device:TPU:2, one launch (start us, length us, event | category | flops | bytes accessed | tf_op | source)
XLA Modules:
  0.0 84.9 jit_solution(11253464941615504378)
XLA Ops:
  0.6 0.0 copy-start
  1.4 0.8 copy.15
  2.2 0.1 select_reduce_fusion
  2.3 0.0 copy-done
  2.4 0.2 bitcast_bitcast_fusion
  2.6 0.2 reshape.133.kv_ref
  2.8 0.0 copy-start.1
  2.8 0.9 %copy-done.1 = bf16[128,1024]{1,0:T(8,128)(2,1)S(1)} copy-done((bf16[128,1024]{1,0:T(8,128)(2,1)S(1)}, bf16[128,1024]{1,0:T(8,128)(2,1)}, u32[]{:S(2)}) %copy-start.1) | copy-done | bytes 262168
  3.7 0.0 copy-start.2
  3.7 0.9 %copy-done.2 = bf16[128,1024]{1,0:T(8,128)(2,1)S(1)} copy-done((bf16[128,1024]{1,0:T(8,128)(2,1)S(1)}, bf16[128,1024]{1,0:T(8,128)(2,1)}, u32[]{:S(2)}) %copy-start.2) | copy-done | bytes 262168
  4.7 77.9 %shard_map.85 = (bf16[128,1024]{1,0:T(8,128)(2,1)S(1)}, bf16[128,1024]{1,0:T(8,128)(2,1)S(1)}, bf16[8,2,32,256]{3,2,1,0:T(8,128)(2,1)S(1)}) custom-call(s32[8,32]{1,0:T(8,128)S(1)} %fusion.6.ids_ref, s32[8,128]{1,0:T(8,128)S(1)} %broadcast_add_fusion.inv_ref, s32[1]{0:T(128)S(6)} %copy.24.len_ref, bf16[128,1024]{1,0:T(8,128)(2,1)S(1)} %copy-done.1, ...), custom_call_target="tpu_custom_call" | custom-call | tf_op jit(solution)/shard_map/pallas_call | solution.py:546
  82.6 0.1 reshape.134
  82.6 0.9 %copy_bitcast_fusion = bf16[2,32,2,1024]{3,2,1,0:T(2,128)(2,1)} fusion(bf16[8,2,32,2,128]{4,3,2,1,0:T(2,128)(2,1)S(1)} %reshape.134), kind=kLoop, calls=%fused_computation | loop fusion | bytes 524288 | tf_op jit(solution)/shard_map/reshape | solution.py:602
  83.5 0.7 copy.25
  84.2 0.7 copy.26
  (4 shorter events, 0.0 us)
Async XLA Ops:
  0.6 1.7 %copy-start = (bf16[2,32,2,1024]{3,2,1,0:T(2,128)(2,1)S(1)}, bf16[2,32,2,1024]{3,2,1,0:T(2,128)(2,1)}, u32[]{:S(2)}) copy-start(bf16[2,32,2,1024]{3,2,1,0:T(2,128)(2,1)} %param.7) | copy-start | bytes 786436
  2.8 1.0 %copy-start.1 = (bf16[128,1024]{1,0:T(8,128)(2,1)S(1)}, bf16[128,1024]{1,0:T(8,128)(2,1)}, u32[]{:S(2)}) copy-start(bf16[128,1024]{1,0:T(8,128)(2,1)} %q_ref.1) | copy-start | bytes 786436
  3.7 0.9 %copy-start.2 = (bf16[128,1024]{1,0:T(8,128)(2,1)S(1)}, bf16[128,1024]{1,0:T(8,128)(2,1)}, u32[]{:S(2)}) copy-start(bf16[128,1024]{1,0:T(8,128)(2,1)} %cot_ref.1) | copy-start | bytes 786436

commit v2 on v1

--- a/solution.py
+++ b/solution.py
@@ -59,7 +59,6 @@
     cxr,
     ysend,
     yrecv,
-    ysum,
     zsend,
     loc_sem,
     kz_s,
@@ -91,7 +90,7 @@
     rows = q_ref.shape[0]
     cols = q_ref.shape[1]
     pdev, plen, width = kv_ref.shape[1:]
-    slots = ids_ref.shape[1]
+    slots = ids_ref.shape[0]
     keys = slots * plen
     chunks = min(CHUNKS, nz)
     zper = nz // chunks
@@ -192,11 +191,17 @@
     def a_copy(xt, xs):
         return remote(asend.at[xt], arecv.at[xs], a_s.at[xt], a_r.at[xs], (me, xt))
 
-    def e_copy(yt):
-        return remote(cxs.at[yt], cxr.at[yt], e_s.at[yt], e_r.at[yt], (at(y, z, oc), x))
-
-    def f_copy(yt, ys):
-        return remote(ysend.at[yt], yrecv.at[ys], f_s.at[yt], f_r.at[ys], (at(yt, z, c), x))
+    def e_copy(i):
+        return remote(cxs.at[i], cxr.at[i], e_s.at[i], e_r.at[i], (at(y, z, oc), x))
+
+    def f_copy(yt, ys, i):
+        return remote(
+            ysend.at[yt, i],
+            yrecv.at[ys, i],
+            f_s.at[yt * chunks + i],
+            f_r.at[ys * chunks + i],
+            (at(yt, z, c), x),
+        )
 
     def o_copy(zt, zs):
         return remote(zsend.at[zt], gkv_ref.at[zs], o_s.at[zt], o_r.at[zs], (at(y, zt, c), x))
@@ -223,11 +228,6 @@
     cot_own.start()
     q_own.start()
     w_load.start()
-    pl.semaphore_wait(barrier, nz + ny + nx - 2)
-
-    each(1, nx, lambda t: x_copy(xat(t), x).start())
-    each(1, nz, lambda t: kz_copy(zat(t), z).start())
-    each(1, nz, lambda t: q_copy(zat(t), z).start())
 
     live = lax.broadcasted_iota(jnp.int32, (rows, 1), 0) < len_ref[0]
     low_lane = lax.broadcasted_iota(jnp.int32, (1, PAIR), 1) < HS
@@ -260,6 +260,9 @@
         each(0, cols // step, one)
 
     grad_part(x, True)
+    pl.semaphore_wait(barrier, nz + ny + nx - 2)
+    each(1, nx, lambda t: x_copy(xat(t), x).start())
+    each(1, nz, lambda t: kz_copy(zat(t), z).start())
 
     kv_own.wait()
 
@@ -276,6 +279,7 @@
         kc_copy(y, c, i).start()
 
     each(0, chunks, forward)
+    each(1, nz, lambda t: q_copy(zat(t), z).start())
 
     def other_part(t):
         xs = xat(t)
@@ -317,26 +321,21 @@
     def pick(wide):
         return jnp.where(low_row, wide[:, :rows], wide[:, rows:])
 
-    def attend(t):
+    def attend(t, lane):
         j = zat(t)
-
-        @pl.when(t > 0)
-        def _():
-            q_copy(j, j).wait_recv()
-
         for k in range(slots):
-            kvg[j, k * plen : (k + 1) * plen, :] = kvbuf[ids_ref[j, k]]
+            kvg[j, k * plen : (k + 1) * plen, :] = kvbuf[ids_ref[k, j]]
         query = both_rows(qbuf[j])
         top = jnp.full((1, 2 * rows), -jnp.inf, jnp.float32)
         for r in range(tiles):
             at_r = pl.ds(r * tile, tile)
             part = dot(kvg[j, at_r, :PAIR], query, NT)
-            stbuf[at_r, :] = part
+            stbuf[lane, at_r, :] = part
             top = jnp.maximum(top, jnp.max(part, axis=0, keepdims=True))
         total = jnp.zeros((1, 2 * rows), jnp.float32)
         for r in range(tiles):
             at_r = pl.ds(r * tile, tile)
-            raised = jnp.exp(stbuf[at_r, :] - top)
+            raised = jnp.exp(stbuf[lane, at_r, :] - top)
             total = total + jnp.sum(raised, axis=0, keepdims=True)
             ebuf[j, at_r, :] = raised.astype(jnp.bfloat16)
         inverse = 1.0 / total
@@ -346,20 +345,29 @@
         invl[j] = inverse
         csend[j] = mixed.T.astype(jnp.bfloat16)
 
-        @pl.when(t > 0)
-        def _():
-            c_copy(j, z).start()
-
-    each(0, nz, attend)
+    def two(wait, work, send):
+        def body(u):
+            for t in (2 * u, 2 * u + 1):
+
+                @pl.when(t > 0)
+                def _():
+                    wait(zat(t))
+
+            for r in range(2):
+                work(2 * u + r, r)
+            for t in (2 * u, 2 * u + 1):
+
+                @pl.when(t > 0)
+                def _():
+                    send(zat(t))
+
+        each(0, nz // 2, body)
+
+    two(lambda j: q_copy(j, j).wait_recv(), attend, lambda j: c_copy(j, z).start())
     ctxbuf[:, lanes(z)] = csend[z]
 
-    def grads(t):
+    def grads(t, lane):
         j = zat(t)
-
-        @pl.when(t > 0)
-        def _():
-            g_copy(j, j).wait_recv()
-
         query = both_rows(qbuf[j])
         inverse = jnp.where(low_row, invl[j, :, :rows], invl[j, :, rows:])
         scaled = gbuf[j].astype(jnp.float32).T * inverse
@@ -377,22 +385,17 @@
             raised = ebuf[j, at_r, :]
             grad = dot(kvg[j, at_r, PAIR:], wide, NN)
             grad = (raised.astype(jnp.float32) * (grad - delta)).astype(jnp.bfloat16)
-            dsbuf[at_r, :] = grad
+            dsbuf[lane, at_r, :] = grad
             per = tile // plen
             key_grad = dot(grad, query, NN).astype(jnp.bfloat16)
             value_grad = dot(raised, wide, NT).astype(jnp.bfloat16)
             sg[j, r * per : (r + 1) * per, :, :PAIR] = key_grad.reshape(per, plen, PAIR)
             sg[j, r * per : (r + 1) * per, :, PAIR:] = value_grad.reshape(per, plen, PAIR)
-        back = pick(dot(kvg[j, :, :PAIR], dsbuf[...], TN))
+        back = pick(dot(kvg[j, :, :PAIR], dsbuf[lane], TN))
         qsend[j] = back.T.astype(jnp.bfloat16)
 
-        @pl.when(t > 0)
-        def _():
-            d_copy(j, z).start()
-
-    each(0, nz // 2, grads)
-
-    each(1, nz, lambda t: c_copy(zat(t), zat(t)).wait_recv())
+    two(lambda j: g_copy(j, j).wait_recv(), grads, lambda j: d_copy(j, z).start())
+    gq_own.start()
 
     def project(xt, own):
         def one(n):
@@ -411,71 +414,65 @@
         project(xt, False)
         a_copy(xt, x).start()
 
-    each(1, nx, project_other)
-    project(x, True)
-    each(nz // 2, nz, grads)
-    gq_own.start()
-
     def gather(p):
         total = sg[0, inv_ref[0, p]].astype(jnp.float32)
         for j in range(1, nz):
             total = total + sg[j, inv_ref[j, p]].astype(jnp.float32)
         return total
 
-    per_y = nz * pdev
-
-    def for_other_core(t):
-        yt = yat(ny - 1 - t)
+    per = zper * pdev
+
+    def for_other_core(i):
+        def one(yt):
+            for k in range(per):
+                cxs[i, yt * per + k] = gather(place(yt, oc, i * zper) + k).astype(jnp.bfloat16)
+
+        each(0, ny, one)
+        e_copy(i).start()
+
+    def for_other_y(i):
+        e_copy(i).wait_recv()
+
+        def one(yt):
+            for k in range(per):
+                total = gather(place(yt, c, i * zper) + k) + cxr[i, yt * per + k].astype(jnp.float32)
+                ysend[yt, i, k] = total.astype(jnp.bfloat16)
+
+        each(0, ny, one)
+        each(1, ny, lambda t: f_copy(yat(t), y, i).start())
+
+    each(0, chunks, for_other_core)
+    each(1, nz, lambda t: c_copy(zat(t), zat(t)).wait_recv())
+    each(1, 2, project_other)
+    each(0, chunks, for_other_y)
+    each(2, nx, project_other)
+
+    def finish(i):
+        each(1, ny, lambda t: f_copy(yat(t), yat(t), i).wait_recv())
 
         def one(k):
-            cxs[yt, k] = gather(place(yt, oc, 0) + k).astype(jnp.bfloat16)
-
-        each(0, per_y, one)
-        e_copy(yt).start()
-
-    each(0, ny, for_other_core)
-
-    def for_other_y(t):
-        yt = yat(t)
-        e_copy(yt).wait_recv()
-
-        def one(k):
-            total = gather(place(yt, c, 0) + k) + cxr[yt, k].astype(jnp.float32)
-            ysend[yt, k] = total.astype(jnp.bfloat16)
-
-        each(0, per_y, one)
-        f_copy(yt, y).start()
-
-    each(1, ny, for_other_y)
-    e_copy(y).wait_recv()
-
-    def own_y(k):
-        ysum[k] = gather(place(y, c, 0) + k) + cxr[y, k].astype(jnp.float32)
-
-    each(0, per_y, own_y)
-
+            zt = i * zper + k
+            for r in range(pdev):
+                total = ysend[y, i, k * pdev + r].astype(jnp.float32)
+                for s in range(1, ny):
+                    total = total + yrecv[yat(s), i, k * pdev + r].astype(jnp.float32)
+                zsend[zt, r] = total.astype(jnp.bfloat16)
+
+            @pl.when(zt != z)
+            def _():
+                o_copy(zt, z).start()
+
+        each(0, zper, one)
+
+    each(0, chunks, finish)
+    gkv_own.start()
+
+    project(x, True)
     each(1, nx, lambda t: a_copy(xat(t), xat(t)).wait_recv())
     out = aown[...]
     for t in range(1, nx):
         out = out + arecv[xat(t)].astype(jnp.float32)
     att_ref[...] = out.astype(jnp.bfloat16)
-
-    each(1, ny, lambda t: f_copy(yat(t), yat(t)).wait_recv())
-
-    def finish(t):
-        zt = zat(t)
-        for k in range(pdev):
-            total = ysum[zt * pdev + k]
-            for s in range(1, ny):
-                total = total + yrecv[yat(s), zt * pdev + k].astype(jnp.float32)
-            zsend[zt, k] = total.astype(jnp.bfloat16)
-
-        @pl.when(t > 0)
-        def _():
-            o_copy(zt, z).start()
-
-    each(0, nz, lambda t: finish(nz - 1 - t))
-    gkv_own.start()
 
     gq_own.wait()
     gkv_own.wait()
@@ -495,11 +492,11 @@
 
     def settle_y(t):
         each(0, chunks, lambda i: ky_copy(yat(t), y, i).wait_send())
-        f_copy(yat(t), y).wait_send()
+        each(0, chunks, lambda i: f_copy(yat(t), y, i).wait_send())
 
     each(1, ny, settle_y)
     each(0, ny * chunks, lambda k: kc_copy(k // chunks, c, lax.rem(k, chunks)).wait_send())
-    each(0, ny, lambda t: e_copy(t).wait_send())
+    each(0, chunks, lambda i: e_copy(i).wait_send())
 
     def settle_x(t):
         x_copy(xat(t), x).wait_send()
@@ -522,16 +519,16 @@
     keys = slots * plen
 
     own = lax.dynamic_slice(
-        retrieval.reshape(ny, nz, CORES, slots),
-        (me // (nz * CORES), 0, me % CORES, 0),
-        (1, nz, 1, slots),
-    ).reshape(nz, slots)
+        retrieval.T.reshape(slots, ny, nz, CORES),
+        (0, me // (nz * CORES), 0, me % CORES),
+        (slots, 1, nz, 1),
+    ).reshape(slots, nz)
     holder = own // pdev
     hy, hz, hc = holder // (nz * CORES), (holder // CORES) % nz, holder % CORES
     ids = ((hy * CORES + hc) * nz + hz) * pdev + own % pdev
     match = ids[:, :, None] == jnp.arange(passages)[None, None, :]
     inverse = slots + jnp.sum(
-        jnp.where(match, jnp.arange(slots)[None, :, None] - slots, 0), axis=1
+        jnp.where(match, jnp.arange(slots)[:, None, None] - slots, 0), axis=0
     )
     pairs = (
         keys_values.reshape(pdev, plen, 2, nz, PAIR)
@@ -551,7 +548,7 @@
             jax.ShapeDtypeStruct((nz, pdev, plen, 2 * PAIR), bf),
         ),
         in_specs=[pl.BlockSpec(memory_space=pltpu.SMEM)] * 3
-        + [pl.BlockSpec(memory_space=pl.ANY)] * 4,
+        + [pl.BlockSpec(memory_space=pltpu.HBM)] * 4,
         out_specs=(
             pl.BlockSpec(memory_space=pltpu.VMEM),
             pl.BlockSpec(memory_space=pl.ANY),
@@ -567,8 +564,8 @@
             vmem((nz, rows, PAIR), bf),
             vmem((nz, keys, 2 * PAIR), bf),
             vmem((nz, keys, 2 * rows), bf),
-            vmem((keys, 2 * rows), bf),
-            vmem((keys, 2 * rows), f32),
+            vmem((2, keys, 2 * rows), bf),
+            vmem((2, keys, 2 * rows), f32),
             vmem((nz, PAIR, rows), f32),
             vmem((nz, 1, 2 * rows), f32),
             vmem((nz, rows, PAIR), bf),
@@ -578,11 +575,10 @@
             vmem((nx, rows, cols), bf),
             vmem((nx, rows, cols), bf),
             vmem((rows, cols), f32),
-            vmem((ny, nz * pdev, plen, 2 * PAIR), bf),
-            vmem((ny, nz * pdev, plen, 2 * PAIR), bf),
-            vmem((ny, nz * pdev, plen, 2 * PAIR), bf),
-            vmem((ny, nz * pdev, plen, 2 * PAIR), bf),
-            vmem((nz * pdev, plen, 2 * PAIR), f32),
+            vmem((chunks, ny * nz * pdev // chunks, plen, 2 * PAIR), bf),
+            vmem((chunks, ny * nz * pdev // chunks, plen, 2 * PAIR), bf),
+            vmem((ny, chunks, nz * pdev // chunks, plen, 2 * PAIR), bf),
+            vmem((ny, chunks, nz * pdev // chunks, plen, 2 * PAIR), bf),
             vmem((nz, pdev, plen, 2 * PAIR), bf),
             dma((6,)),
         ]
@@ -590,7 +586,8 @@
         + [dma((ny * chunks,))] * 4
         + [dma((nz,))] * 8
         + [dma((nx,))] * 4
-        + [dma((ny,))] * 4
+        + [dma((chunks,))] * 2
+        + [dma((ny * chunks,))] * 2
         + [dma((nz,))] * 2,
         compiler_params=pltpu.CompilerParams(
             collective_id=0, has_side_effects=True, vmem_limit_bytes=48 * 1024 * 1024

time: 86.3 us -> 74.8 us (0.87)
  Pallas kernels: 77.9 us -> 66.2 us
    pallas_call x1, Pallas kernels: 77.9 us -> 66.2 us  [local(): pl.pallas_call(functools.partial(kernel, nx, ny, nz), out_shape=(jax.Shap...]
where the time goes in v2:
time: 74.8 us; the launch traced here: 73.4 us
  Pallas kernels  66.2 us (89%)
  local copies, waits for them, and re-layouts  5.55 us (7%)
  between operations  1.43 us (2%)
    pallas_call x1, Pallas kernels, local(): pl.pallas_call(functools.partial(kernel, nx, ny, nz), out_shape=(jax.Shap...  66.2 us
    unnamed x9, local copies, waits for them, and re-layouts  4.11 us

profile of v2, /device:TPU:2, one launch (start us, length us, event | category | flops | bytes accessed | tf_op | source)
XLA Modules:
  0.0 73.4 jit_solution(12538677136276684185)
XLA Ops:
  0.6 0.0 copy-start
  1.4 0.8 %copy.16 = s32[64,32]{1,0:T(8,128)S(1)} copy(s32[64,32]{0,1:T(8,128)} %param.10) | data formatting | bytes 16384 | tf_op args[4]
  2.2 0.1 copy.17
  2.3 0.1 fusion.6.ids_ref
  2.3 0.1 select_reduce_fusion
  2.5 0.0 copy-done
  2.5 0.2 bitcast_bitcast_fusion
  2.7 0.2 reshape.133.kv_ref
  2.9 0.0 copy-start.1
  2.9 0.9 %copy-done.1 = bf16[128,1024]{1,0:T(8,128)(2,1)S(1)} copy-done((bf16[128,1024]{1,0:T(8,128)(2,1)S(1)}, bf16[128,1024]{1,0:T(8,128)(2,1)}, u32[]{:S(2)}) %copy-start.1) | copy-done | bytes 262168
  3.9 0.0 copy-start.2
  3.9 0.9 %copy-done.2 = bf16[128,1024]{1,0:T(8,128)(2,1)S(1)} copy-done((bf16[128,1024]{1,0:T(8,128)(2,1)S(1)}, bf16[128,1024]{1,0:T(8,128)(2,1)}, u32[]{:S(2)}) %copy-start.2) | copy-done | bytes 262168
  4.8 66.2 %shard_map.85 = (bf16[128,1024]{1,0:T(8,128)(2,1)S(1)}, bf16[128,1024]{1,0:T(8,128)(2,1)S(1)}, bf16[8,2,32,256]{3,2,1,0:T(8,128)(2,1)S(1)}) custom-call(s32[32,8]{1,0:T(8,128)S(1)} %fusion.6.ids_ref, s32[8,128]{1,0:T(8,128)S(1)} %broadcast_add_fusion.inv_ref, s32[1]{0:T(128)S(6)} %copy.26.len_ref, bf16[128,1024]{1,0:T(8,128)(2,1)S(1)} %copy-done.1, ...), custom_call_target="tpu_custom_call" | custom-call | tf_op jit(solution)/shard_map/pallas_call | solution.py:543
  71.0 0.1 reshape.134
  71.1 0.9 %copy_bitcast_fusion = bf16[2,32,2,1024]{3,2,1,0:T(2,128)(2,1)} fusion(bf16[8,2,32,2,128]{4,3,2,1,0:T(2,128)(2,1)S(1)} %reshape.134), kind=kLoop, calls=%fused_computation | loop fusion | bytes 524288 | tf_op jit(solution)/shard_map/reshape | solution.py:599
  72.0 0.7 copy.27
  72.7 0.7 copy.28
  (3 shorter events, 0.0 us)
Async XLA Ops:
  0.6 1.8 %copy-start = (bf16[2,32,2,1024]{3,2,1,0:T(2,128)(2,1)S(1)}, bf16[2,32,2,1024]{3,2,1,0:T(2,128)(2,1)}, u32[]{:S(2)}) copy-start(bf16[2,32,2,1024]{3,2,1,0:T(2,128)(2,1)} %param.7) | copy-start | bytes 786436
  2.9 1.0 %copy-start.1 = (bf16[128,1024]{1,0:T(8,128)(2,1)S(1)}, bf16[128,1024]{1,0:T(8,128)(2,1)}, u32[]{:S(2)}) copy-start(bf16[128,1024]{1,0:T(8,128)(2,1)} %q_ref.1) | copy-start | bytes 786436
  3.9 0.9 %copy-start.2 = (bf16[128,1024]{1,0:T(8,128)(2,1)S(1)}, bf16[128,1024]{1,0:T(8,128)(2,1)}, u32[]{:S(2)}) copy-start(bf16[128,1024]{1,0:T(8,128)(2,1)} %cot_ref.1) | copy-start | bytes 786436

commit v3 on v2

--- a/solution.py
+++ b/solution.py
@@ -11,6 +11,7 @@
 PAIR = 2 * HS
 CORES = 2
 CHUNKS = 4
+AT_ONCE = 4
 MESH = pl.DeviceIdType.MESH
 NT = (((1,), (1,)), ((), ()))
 TN = (((0,), (0,)), ((), ()))
@@ -59,6 +60,7 @@
     cxr,
     ysend,
     yrecv,
+    yrelay,
     zsend,
     loc_sem,
     kz_s,
@@ -83,6 +85,8 @@
     e_r,
     f_s,
     f_r,
+    r_s,
+    r_r,
     o_s,
     o_r,
 ):
@@ -94,6 +98,7 @@
     keys = slots * plen
     chunks = min(CHUNKS, nz)
     zper = nz // chunks
+    wide_step = min(AT_ONCE, nz)
     me = lax.axis_index("pass")
     x = lax.axis_index("tensor")
     c = lax.rem(me, nc)
@@ -194,6 +199,9 @@
     def e_copy(i):
         return remote(cxs.at[i], cxr.at[i], e_s.at[i], e_r.at[i], (at(y, z, oc), x))
 
+    def ahead(i):
+        return 1 - 2 * lax.rem(i, 2)
+
     def f_copy(yt, ys, i):
         return remote(
             ysend.at[yt, i],
@@ -201,6 +209,15 @@
             f_s.at[yt * chunks + i],
             f_r.at[ys * chunks + i],
             (at(yt, z, c), x),
+        )
+
+    def r_copy(i):
+        return remote(
+            ysend.at[lax.rem(y + 2, ny), i],
+            yrelay.at[i],
+            r_s.at[i],
+            r_r.at[i],
+            (at(lax.rem(y + ahead(i) + ny, ny), z, c), x),
         )
 
     def o_copy(zt, zs):
@@ -278,19 +295,37 @@
         each(1, ny, lambda t: ky_copy(yat(t), y, i).start())
         kc_copy(y, c, i).start()
 
-    each(0, chunks, forward)
+    forward(0)
     each(1, nz, lambda t: q_copy(zat(t), z).start())
+    each(1, chunks, forward)
 
     def other_part(t):
         xs = xat(t)
         x_copy(xs, xs).wait_recv()
         grad_part(xs, False)
 
-    each(1, nx, other_part)
-    for h in range(nz):
-        gsend[h] = jnp.where(live, gacc[:, h * PAIR : (h + 1) * PAIR], 0.0).astype(jnp.bfloat16)
+    if nx > 1:
+        each(1, nx - 1, other_part)
+        xs = xat(nx - 1)
+        x_copy(xs, xs).wait_recv()
+
+    def last_part(n):
+        at_n = pl.ds(pl.multiple_of(n * step, step), step)
+        part = gacc[:, at_n]
+        if nx > 1:
+            weight = wbuf[at_n, pl.ds(pl.multiple_of(xs * cols, cols), cols)]
+            part = part + dot(cotbuf[xs], weight, NT)
+        part = jnp.where(live, part, 0.0).astype(jnp.bfloat16)
+        for k in range(step // PAIR):
+            h = n * (step // PAIR) + k
+            gsend[h] = part[:, k * PAIR : (k + 1) * PAIR]
+
+            @pl.when(h != z)
+            def _():
+                g_copy(h, z).start()
+
+    each(0, cols // step, last_part)
     gbuf[z] = gsend[z]
-    each(1, nz, lambda t: g_copy(zat(t), z).start())
 
     def pass_on(t):
         ys = yat(t)
@@ -345,25 +380,25 @@
         invl[j] = inverse
         csend[j] = mixed.T.astype(jnp.bfloat16)
 
-    def two(wait, work, send):
+    def batches(wait, work, send):
         def body(u):
-            for t in (2 * u, 2 * u + 1):
+            for t in [wide_step * u + r for r in range(wide_step)]:
 
                 @pl.when(t > 0)
                 def _():
                     wait(zat(t))
 
-            for r in range(2):
-                work(2 * u + r, r)
-            for t in (2 * u, 2 * u + 1):
+            for r in range(wide_step):
+                work(wide_step * u + r, r)
+            for t in [wide_step * u + r for r in range(wide_step)]:
 
                 @pl.when(t > 0)
                 def _():
                     send(zat(t))
 
-        each(0, nz // 2, body)
-
-    two(lambda j: q_copy(j, j).wait_recv(), attend, lambda j: c_copy(j, z).start())
+        each(0, nz // wide_step, body)
+
+    batches(lambda j: q_copy(j, j).wait_recv(), attend, lambda j: c_copy(j, z).start())
     ctxbuf[:, lanes(z)] = csend[z]
 
     def grads(t, lane):
@@ -394,7 +429,7 @@
         back = pick(dot(kvg[j, :, :PAIR], dsbuf[lane], TN))
         qsend[j] = back.T.astype(jnp.bfloat16)
 
-    two(lambda j: g_copy(j, j).wait_recv(), grads, lambda j: d_copy(j, z).start())
+    batches(lambda j: g_copy(j, j).wait_recv(), grads, lambda j: d_copy(j, z).start())
     gq_own.start()
 
     def project(xt, own):
@@ -439,22 +474,39 @@
                 ysend[yt, i, k] = total.astype(jnp.bfloat16)
 
         each(0, ny, one)
-        each(1, ny, lambda t: f_copy(yat(t), y, i).start())
-
-    each(0, chunks, for_other_core)
+        r_copy(i).start()
+        f_copy(lax.rem(y - ahead(i) + ny, ny), y, i).start()
+
+    def relay(i):
+        r_copy(i).wait_recv()
+        yt = lax.rem(y + ahead(i) + ny, ny)
+        for k in range(per):
+            total = ysend[yt, i, k].astype(jnp.float32) + yrelay[i, k].astype(jnp.float32)
+            ysend[yt, i, k] = total.astype(jnp.bfloat16)
+        f_copy(yt, y, i).start()
+
+    def core_then_y(i):
+        for_other_core(i)
+        for_other_y(i - 1)
+
+    for_other_core(0)
+    each(1, chunks, core_then_y)
+    for_other_y(chunks - 1)
     each(1, nz, lambda t: c_copy(zat(t), zat(t)).wait_recv())
-    each(1, 2, project_other)
-    each(0, chunks, for_other_y)
-    each(2, nx, project_other)
+    each(1, min(2, nx), project_other)
+    each(0, chunks // 2, relay)
+    each(2, min(3, nx), project_other)
+    each(chunks // 2, chunks, relay)
+    each(3, nx, project_other)
 
     def finish(i):
-        each(1, ny, lambda t: f_copy(yat(t), yat(t), i).wait_recv())
+        each(1, 3, lambda t: f_copy(yat(t), yat(t), i).wait_recv())
 
         def one(k):
             zt = i * zper + k
             for r in range(pdev):
                 total = ysend[y, i, k * pdev + r].astype(jnp.float32)
-                for s in range(1, ny):
+                for s in range(1, 3):
                     total = total + yrecv[yat(s), i, k * pdev + r].astype(jnp.float32)
                 zsend[zt, r] = total.astype(jnp.bfloat16)
 
@@ -492,11 +544,12 @@
 
     def settle_y(t):
         each(0, chunks, lambda i: ky_copy(yat(t), y, i).wait_send())
-        each(0, chunks, lambda i: f_copy(yat(t), y, i).wait_send())
 
     each(1, ny, settle_y)
     each(0, ny * chunks, lambda k: kc_copy(k // chunks, c, lax.rem(k, chunks)).wait_send())
     each(0, chunks, lambda i: e_copy(i).wait_send())
+    each(0, chunks, lambda i: r_copy(i).wait_send())
+    each(1, 3, lambda t: each(0, chunks, lambda i: f_copy(yat(t), y, i).wait_send()))
 
     def settle_x(t):
         x_copy(xat(t), x).wait_send()
@@ -564,8 +617,8 @@
             vmem((nz, rows, PAIR), bf),
             vmem((nz, keys, 2 * PAIR), bf),
             vmem((nz, keys, 2 * rows), bf),
-            vmem((2, keys, 2 * rows), bf),
-            vmem((2, keys, 2 * rows), f32),
+            vmem((min(AT_ONCE, nz), keys, 2 * rows), bf),
+            vmem((min(AT_ONCE, nz), keys, 2 * rows), f32),
             vmem((nz, PAIR, rows), f32),
             vmem((nz, 1, 2 * rows), f32),
             vmem((nz, rows, PAIR), bf),
@@ -579,6 +632,7 @@
             vmem((chunks, ny * nz * pdev // chunks, plen, 2 * PAIR), bf),
             vmem((ny, chunks, nz * pdev // chunks, plen, 2 * PAIR), bf),
             vmem((ny, chunks, nz * pdev // chunks, plen, 2 * PAIR), bf),
+            vmem((chunks, nz * pdev // chunks, plen, 2 * PAIR), bf),
             vmem((nz, pdev, plen, 2 * PAIR), bf),
             dma((6,)),
         ]
@@ -588,6 +642,7 @@
         + [dma((nx,))] * 4
         + [dma((chunks,))] * 2
         + [dma((ny * chunks,))] * 2
+        + [dma((chunks,))] * 2
         + [dma((nz,))] * 2,
         compiler_params=pltpu.CompilerParams(
             collective_id=0, has_side_effects=True, vmem_limit_bytes=48 * 1024 * 1024

time: 74.8 us -> 73.7 us (0.985); the launches traced: 73.4 us -> 73.3 us
  no operation moved by 1% of the time
where the time goes in v3:
time: 73.7 us; the launch traced here: 73.3 us
  Pallas kernels  66.1 us (90%)
  local copies, waits for them, and re-layouts  5.55 us (8%)
  between operations  1.43 us (2%)
    pallas_call x1, Pallas kernels, local(): pl.pallas_call(functools.partial(kernel, nx, ny, nz), out_shape=(jax.Shap...  66.1 us
    unnamed x9, local copies, waits for them, and re-layouts  4.11 us

profile of v3, /device:TPU:2, one launch (start us, length us, event | category | flops | bytes accessed | tf_op | source)
XLA Modules:
  0.0 73.3 jit_solution(14503879863267783586)
XLA Ops:
  0.6 0.0 copy-start
  1.4 0.8 %copy.16 = s32[64,32]{1,0:T(8,128)S(1)} copy(s32[64,32]{0,1:T(8,128)} %param.10) | data formatting | bytes 16384 | tf_op args[4]
  2.2 0.1 copy.17
  2.3 0.1 fusion.6.ids_ref
  2.3 0.1 select_reduce_fusion
  2.5 0.0 copy-done
  2.5 0.2 bitcast_bitcast_fusion
  2.7 0.2 reshape.133.kv_ref
  2.9 0.0 copy-start.1
  2.9 0.9 %copy-done.1 = bf16[128,1024]{1,0:T(8,128)(2,1)S(1)} copy-done((bf16[128,1024]{1,0:T(8,128)(2,1)S(1)}, bf16[128,1024]{1,0:T(8,128)(2,1)}, u32[]{:S(2)}) %copy-start.1) | copy-done | bytes 262168
  3.9 0.0 copy-start.2
  3.9 0.9 %copy-done.2 = bf16[128,1024]{1,0:T(8,128)(2,1)S(1)} copy-done((bf16[128,1024]{1,0:T(8,128)(2,1)S(1)}, bf16[128,1024]{1,0:T(8,128)(2,1)}, u32[]{:S(2)}) %copy-start.2) | copy-done | bytes 262168
  4.8 66.1 %shard_map.85 = (bf16[128,1024]{1,0:T(8,128)(2,1)S(1)}, bf16[128,1024]{1,0:T(8,128)(2,1)S(1)}, bf16[8,2,32,256]{3,2,1,0:T(8,128)(2,1)S(1)}) custom-call(s32[32,8]{1,0:T(8,128)S(1)} %fusion.6.ids_ref, s32[8,128]{1,0:T(8,128)S(1)} %broadcast_add_fusion.inv_ref, s32[1]{0:T(128)S(6)} %copy.26.len_ref, bf16[128,1024]{1,0:T(8,128)(2,1)S(1)} %copy-done.1, ...), custom_call_target="tpu_custom_call" | custom-call | tf_op jit(solution)/shard_map/pallas_call | solution.py:596
  70.9 0.1 reshape.134
  71.0 0.9 %copy_bitcast_fusion = bf16[2,32,2,1024]{3,2,1,0:T(2,128)(2,1)} fusion(bf16[8,2,32,2,128]{4,3,2,1,0:T(2,128)(2,1)S(1)} %reshape.134), kind=kLoop, calls=%fused_computation | loop fusion | bytes 524288 | tf_op jit(solution)/shard_map/reshape | solution.py:654
  71.9 0.7 copy.27
  72.6 0.7 copy.28
  (3 shorter events, 0.0 us)
Async XLA Ops:
  0.6 1.8 %copy-start = (bf16[2,32,2,1024]{3,2,1,0:T(2,128)(2,1)S(1)}, bf16[2,32,2,1024]{3,2,1,0:T(2,128)(2,1)}, u32[]{:S(2)}) copy-start(bf16[2,32,2,1024]{3,2,1,0:T(2,128)(2,1)} %param.7) | copy-start | bytes 786436
  2.9 1.0 %copy-start.1 = (bf16[128,1024]{1,0:T(8,128)(2,1)S(1)}, bf16[128,1024]{1,0:T(8,128)(2,1)}, u32[]{:S(2)}) copy-start(bf16[128,1024]{1,0:T(8,128)(2,1)} %q_ref.1) | copy-start | bytes 786436
  3.9 0.9 %copy-start.2 = (bf16[128,1024]{1,0:T(8,128)(2,1)S(1)}, bf16[128,1024]{1,0:T(8,128)(2,1)}, u32[]{:S(2)}) copy-start(bf16[128,1024]{1,0:T(8,128)(2,1)} %cot_ref.1) | copy-start | bytes 786436

commit v4 on v3

--- a/solution.py
+++ b/solution.py
@@ -10,7 +10,7 @@
 HS = 64
 PAIR = 2 * HS
 CORES = 2
-CHUNKS = 4
+CHUNKS = 2
 AT_ONCE = 4
 MESH = pl.DeviceIdType.MESH
 NT = (((1,), (1,)), ((), ()))

time: 73.7 us -> 72.7 us (0.986)
  Pallas kernels: 66.1 us -> 64.5 us
    pallas_call x1, Pallas kernels: 66.1 us -> 64.5 us  [local(): pl.pallas_call(functools.partial(kernel, nx, ny, nz), out_shape=(jax.Shap...]
where the time goes in v4:
time: 72.7 us; the launch traced here: 71.7 us
  Pallas kernels  64.5 us (89%)
  local copies, waits for them, and re-layouts  5.55 us (8%)
  between operations  1.43 us (2%)
    pallas_call x1, Pallas kernels, local(): pl.pallas_call(functools.partial(kernel, nx, ny, nz), out_shape=(jax.Shap...  64.5 us
    unnamed x9, local copies, waits for them, and re-layouts  4.11 us

profile of v4, /device:TPU:2, one launch (start us, length us, event | category | flops | bytes accessed | tf_op | source)
XLA Modules:
  0.0 71.7 jit_solution(8217919264908000427)
XLA Ops:
  0.6 0.0 copy-start
  1.4 0.8 %copy.16 = s32[64,32]{1,0:T(8,128)S(1)} copy(s32[64,32]{0,1:T(8,128)} %param.10) | data formatting | bytes 16384 | tf_op args[4]
  2.2 0.1 copy.17
  2.3 0.1 fusion.6.ids_ref
  2.3 0.1 select_reduce_fusion
  2.5 0.0 copy-done
  2.5 0.2 bitcast_bitcast_fusion
  2.7 0.2 reshape.133.kv_ref
  2.9 0.0 copy-start.1
  2.9 0.9 %copy-done.1 = bf16[128,1024]{1,0:T(8,128)(2,1)S(1)} copy-done((bf16[128,1024]{1,0:T(8,128)(2,1)S(1)}, bf16[128,1024]{1,0:T(8,128)(2,1)}, u32[]{:S(2)}) %copy-start.1) | copy-done | bytes 262168
  3.9 0.0 copy-start.2
  3.9 0.9 %copy-done.2 = bf16[128,1024]{1,0:T(8,128)(2,1)S(1)} copy-done((bf16[128,1024]{1,0:T(8,128)(2,1)S(1)}, bf16[128,1024]{1,0:T(8,128)(2,1)}, u32[]{:S(2)}) %copy-start.2) | copy-done | bytes 262168
  4.8 64.5 %shard_map.85 = (bf16[128,1024]{1,0:T(8,128)(2,1)S(1)}, bf16[128,1024]{1,0:T(8,128)(2,1)S(1)}, bf16[8,2,32,256]{3,2,1,0:T(8,128)(2,1)S(1)}) custom-call(s32[32,8]{1,0:T(8,128)S(1)} %fusion.6.ids_ref, s32[8,128]{1,0:T(8,128)S(1)} %broadcast_add_fusion.inv_ref, s32[1]{0:T(128)S(6)} %copy.26.len_ref, bf16[128,1024]{1,0:T(8,128)(2,1)S(1)} %copy-done.1, ...), custom_call_target="tpu_custom_call" | custom-call | tf_op jit(solution)/shard_map/pallas_call | solution.py:596
  69.3 0.1 reshape.134
  69.4 0.9 %copy_bitcast_fusion = bf16[2,32,2,1024]{3,2,1,0:T(2,128)(2,1)} fusion(bf16[8,2,32,2,128]{4,3,2,1,0:T(2,128)(2,1)S(1)} %reshape.134), kind=kLoop, calls=%fused_computation | loop fusion | bytes 524288 | tf_op jit(solution)/shard_map/reshape | solution.py:654
  70.3 0.7 copy.27
  71.0 0.7 copy.28
  (3 shorter events, 0.0 us)
Async XLA Ops:
  0.6 1.8 %copy-start = (bf16[2,32,2,1024]{3,2,1,0:T(2,128)(2,1)S(1)}, bf16[2,32,2,1024]{3,2,1,0:T(2,128)(2,1)}, u32[]{:S(2)}) copy-start(bf16[2,32,2,1024]{3,2,1,0:T(2,128)(2,1)} %param.7) | copy-start | bytes 786436
  2.9 1.0 %copy-start.1 = (bf16[128,1024]{1,0:T(8,128)(2,1)S(1)}, bf16[128,1024]{1,0:T(8,128)(2,1)}, u32[]{:S(2)}) copy-start(bf16[128,1024]{1,0:T(8,128)(2,1)} %q_ref.1) | copy-start | bytes 786436
  3.9 0.9 %copy-start.2 = (bf16[128,1024]{1,0:T(8,128)(2,1)S(1)}, bf16[128,1024]{1,0:T(8,128)(2,1)}, u32[]{:S(2)}) copy-start(bf16[128,1024]{1,0:T(8,128)(2,1)} %cot_ref.1) | copy-start | bytes 786436

commit v5 on v4

--- a/solution.py
+++ b/solution.py
@@ -11,6 +11,7 @@
 PAIR = 2 * HS
 CORES = 2
 CHUNKS = 2
+PARTS = 1
 AT_ONCE = 4
 MESH = pl.DeviceIdType.MESH
 NT = (((1,), (1,)), ((), ()))
@@ -98,6 +99,8 @@
     keys = slots * plen
     chunks = min(CHUNKS, nz)
     zper = nz // chunks
+    parts = min(PARTS, nz)
+    fper = nz // parts
     wide_step = min(AT_ONCE, nz)
     me = lax.axis_index("pass")
     x = lax.axis_index("tensor")
@@ -151,22 +154,22 @@
         )
 
     def ky_copy(yt, ys, i):
-        part = pl.ds(place(ys, c, i * zper), zper * pdev)
+        part = pl.ds(place(ys, c, i * fper), fper * pdev)
         return remote(
             kvbuf.at[part],
             kvbuf.at[part],
-            ky_s.at[yt * chunks + i],
-            ky_r.at[ys * chunks + i],
+            ky_s.at[yt * parts + i],
+            ky_r.at[ys * parts + i],
             (at(yt, z, c), x),
         )
 
     def kc_copy(ys, cs, i):
-        part = pl.ds(place(ys, cs, i * zper), zper * pdev)
+        part = pl.ds(place(ys, cs, i * fper), fper * pdev)
         return remote(
             kvbuf.at[part],
             kvbuf.at[part],
-            kc_s.at[ys * chunks + i],
-            kc_r.at[ys * chunks + i],
+            kc_s.at[ys * parts + i],
+            kc_r.at[ys * parts + i],
             (at(y, z, oc), x),
         )
 
@@ -285,19 +288,19 @@
 
     def forward(i):
         def arrived(k):
-            zs = i * zper + k
+            zs = i * fper + k
 
             @pl.when(zs != z)
             def _():
                 kz_copy(zs, zs).wait_recv()
 
-        each(0, zper, arrived)
+        each(0, fper, arrived)
         each(1, ny, lambda t: ky_copy(yat(t), y, i).start())
         kc_copy(y, c, i).start()
 
     forward(0)
     each(1, nz, lambda t: q_copy(zat(t), z).start())
-    each(1, chunks, forward)
+    each(1, parts, forward)
 
     def other_part(t):
         xs = xat(t)
@@ -334,10 +337,10 @@
             ky_copy(ys, ys, i).wait_recv()
             kc_copy(ys, c, i).start()
 
-        each(0, chunks, one)
+        each(0, parts, one)
 
     each(1, ny, pass_on)
-    each(0, ny * chunks, lambda k: kc_copy(k // chunks, oc, lax.rem(k, chunks)).wait_recv())
+    each(0, ny * parts, lambda k: kc_copy(k // parts, oc, lax.rem(k, parts)).wait_recv())
 
     q_own.wait()
     tile = 256
@@ -543,10 +546,10 @@
     each(1, nz, settle_z)
 
     def settle_y(t):
-        each(0, chunks, lambda i: ky_copy(yat(t), y, i).wait_send())
+        each(0, parts, lambda i: ky_copy(yat(t), y, i).wait_send())
 
     each(1, ny, settle_y)
-    each(0, ny * chunks, lambda k: kc_copy(k // chunks, c, lax.rem(k, chunks)).wait_send())
+    each(0, ny * parts, lambda k: kc_copy(k // parts, c, lax.rem(k, parts)).wait_send())
     each(0, chunks, lambda i: e_copy(i).wait_send())
     each(0, chunks, lambda i: r_copy(i).wait_send())
     each(1, 3, lambda t: each(0, chunks, lambda i: f_copy(yat(t), y, i).wait_send()))

time: 72.7 us -> 77.3 us (1.063); the launches traced: 71.7 us -> 77.1 us
  Pallas kernels: 64.5 us -> 69.9 us
    pallas_call x1, Pallas kernels: 64.5 us -> 69.9 us  [local(): pl.pallas_call(functools.partial(kernel, nx, ny, nz), out_shape=(jax.Shap...]
where the time goes in v5:
time: 77.3 us; the launch traced here: 77.1 us
  Pallas kernels  69.9 us (90%)
  local copies, waits for them, and re-layouts  5.55 us (7%)
  between operations  1.43 us (2%)
    pallas_call x1, Pallas kernels, local(): pl.pallas_call(functools.partial(kernel, nx, ny, nz), out_shape=(jax.Shap...  69.9 us
    unnamed x9, local copies, waits for them, and re-layouts  4.11 us

profile of v5, /device:TPU:2, one launch (start us, length us, event | category | flops | bytes accessed | tf_op | source)
XLA Modules:
  0.0 77.1 jit_solution(11760243213220544627)
XLA Ops:
  0.6 0.0 copy-start
  1.4 0.8 %copy.16 = s32[64,32]{1,0:T(8,128)S(1)} copy(s32[64,32]{0,1:T(8,128)} %param.10) | data formatting | bytes 16384 | tf_op args[4]
  2.2 0.1 copy.17
  2.3 0.1 fusion.6.ids_ref
  2.3 0.1 select_reduce_fusion
  2.5 0.0 copy-done
  2.5 0.2 bitcast_bitcast_fusion
  2.7 0.2 reshape.133.kv_ref
  2.9 0.0 copy-start.1
  2.9 0.9 %copy-done.1 = bf16[128,1024]{1,0:T(8,128)(2,1)S(1)} copy-done((bf16[128,1024]{1,0:T(8,128)(2,1)S(1)}, bf16[128,1024]{1,0:T(8,128)(2,1)}, u32[]{:S(2)}) %copy-start.1) | copy-done | bytes 262168
  3.9 0.0 copy-start.2
  3.9 0.9 %copy-done.2 = bf16[128,1024]{1,0:T(8,128)(2,1)S(1)} copy-done((bf16[128,1024]{1,0:T(8,128)(2,1)S(1)}, bf16[128,1024]{1,0:T(8,128)(2,1)}, u32[]{:S(2)}) %copy-start.2) | copy-done | bytes 262168
  4.8 69.9 %shard_map.85 = (bf16[128,1024]{1,0:T(8,128)(2,1)S(1)}, bf16[128,1024]{1,0:T(8,128)(2,1)S(1)}, bf16[8,2,32,256]{3,2,1,0:T(8,128)(2,1)S(1)}) custom-call(s32[32,8]{1,0:T(8,128)S(1)} %fusion.6.ids_ref, s32[8,128]{1,0:T(8,128)S(1)} %broadcast_add_fusion.inv_ref, s32[1]{0:T(128)S(6)} %copy.26.len_ref, bf16[128,1024]{1,0:T(8,128)(2,1)S(1)} %copy-done.1, ...), custom_call_target="tpu_custom_call" | custom-call | tf_op jit(solution)/shard_map/pallas_call | solution.py:599
  74.7 0.1 reshape.134
  74.8 0.9 %copy_bitcast_fusion = bf16[2,32,2,1024]{3,2,1,0:T(2,128)(2,1)} fusion(bf16[8,2,32,2,128]{4,3,2,1,0:T(2,128)(2,1)S(1)} %reshape.134), kind=kLoop, calls=%fused_computation | loop fusion | bytes 524288 | tf_op jit(solution)/shard_map/reshape | solution.py:657
  75.7 0.7 copy.27
  76.4 0.7 copy.28
  (3 shorter events, 0.0 us)
Async XLA Ops:
  0.6 1.8 %copy-start = (bf16[2,32,2,1024]{3,2,1,0:T(2,128)(2,1)S(1)}, bf16[2,32,2,1024]{3,2,1,0:T(2,128)(2,1)}, u32[]{:S(2)}) copy-start(bf16[2,32,2,1024]{3,2,1,0:T(2,128)(2,1)} %param.7) | copy-start | bytes 786436
  2.9 1.0 %copy-start.1 = (bf16[128,1024]{1,0:T(8,128)(2,1)S(1)}, bf16[128,1024]{1,0:T(8,128)(2,1)}, u32[]{:S(2)}) copy-start(bf16[128,1024]{1,0:T(8,128)(2,1)} %q_ref.1) | copy-start | bytes 786436
  3.9 0.9 %copy-start.2 = (bf16[128,1024]{1,0:T(8,128)(2,1)S(1)}, bf16[128,1024]{1,0:T(8,128)(2,1)}, u32[]{:S(2)}) copy-start(bf16[128,1024]{1,0:T(8,128)(2,1)} %cot_ref.1) | copy-start | bytes 786436
